TPU v7x, 512 devices: a whole 4x8x8 slice. The times are simulated.
512 devices in a mesh: trow: 8 (over y), tcol: 8 (over x, z_lo), dp: 8 (over z_hi, core).
Axes of the slice: x: 4, y: 8, z: 8 (z_hi: 4, z_lo: 2; z = z_hi * 2 + z_lo), core: 2. Of those that a mesh axis runs over, the one named last changes fastest.
Arguments:
- embeds: bfloat16 [8192, 1024], P('dp'), may hold values from -6 to 6
- frequencies: bfloat16 [1024, 8192], P(None, ('trow', 'tcol')), may hold values from -0.5 to 0.5
- phases: float32 [8192], P(('trow', 'tcol')), may hold values from -3.140625 to 3.140625
- labels: int32 [8192], P('dp'), may hold values from 0 to 999
- weights: float32 [8192, 1000], P(('tcol', 'dp'), 'trow'), may hold values from -6 to 6
Outputs:
- gram_matrix: float32 [8192, 8192], P(('trow', 'dp'), 'tcol')
- new_weights: float32 [8192, 1000], P(('tcol', 'dp'), 'trow')
All inputs are finite; a program needn't handle non-finite values.
Results may differ from a plain program's by a relative error of at most 0.023.
Values may be sent and summed in bfloat16 or wider, within the bound.
A program may use at most 64 MiB of HBM per device.

v0:
```python
import jax
import jax.numpy as jnp
from jax import lax
from jax.sharding import PartitionSpec as P

C = 1000
ROOT_TWO = 1.4142135623730951
RIDGE = 0.5
STEP_RATE = 0.5


def copy_for_each(array, axis):
    size = lax.axis_size(axis)
    return lax.all_to_all(
        jnp.broadcast_to(array[None], (size, *array.shape)), axis, 0, 0, tiled=True
    )


def laid_out(parts, dim):
    dims = list(parts.shape[1:])
    dims[dim] *= parts.shape[0]
    return jnp.moveaxis(parts, 0, dim).reshape(dims)


def gather_directly(array, axis, dim):
    parts = copy_for_each(array, axis)
    return laid_out(parts, dim)


def padded_to(lines, size):
    spare = -lines.shape[0] % size
    if not spare:
        return lines
    return jnp.concatenate([lines, jnp.zeros((spare, *lines.shape[1:]), lines.dtype)])


def broadcast_by_parts(array, axis, root):
    lines = jnp.where(lax.axis_index(axis) == root, array, jnp.zeros_like(array)).reshape(
        -1, *array.shape[1:][-1:]
    )
    padded = padded_to(lines, lax.axis_size(axis))
    own = lax.psum_scatter(padded, axis, scatter_dimension=0, tiled=True)
    return lax.all_gather(own, axis, axis=0, tiled=True)[: len(lines)].reshape(array.shape)


def split_up(array, dim, size):
    dims = array.shape
    parts = array.reshape(*dims[:dim], size, dims[dim] // size, *dims[dim + 1 :])
    return jnp.moveaxis(parts, dim, 0)


def sum_at_owner(array, axis, dim):
    parts = split_up(array, dim, lax.axis_size(axis))
    arrived = lax.all_to_all(parts, axis, split_axis=0, concat_axis=0, tiled=True)
    return arrived.astype(jnp.float32).sum(axis=0)


def of_everyone(array, axis):
    everything = copy_for_each(array, axis)
    return jnp.sum(everything.astype(jnp.float32), axis=0)


def broadcast(array, axis, root):
    return lax.dynamic_index_in_dim(lax.all_gather(array, axis), root, 0, keepdims=False)


def featurize(embeds, frequencies, phases):
    angles = jnp.dot(embeds, frequencies, preferred_element_type=jnp.float32) + phases
    return (ROOT_TWO * jnp.cos(angles)).astype(jnp.bfloat16)


def shards(embeds, frequencies, phases, labels, weights):
    rows_here = embeds.shape[0]
    n_row = lax.axis_size("trow")
    n_dp = lax.axis_size("dp")
    row_idx = lax.axis_index("trow")
    col_idx = lax.axis_index("tcol")
    dp_idx = lax.axis_index("dp")
    total_rows = rows_here * n_dp
    contract = (((0,), (0,)), ((), ()))
    own_part = featurize(embeds, frequencies, phases)
    left_feats = gather_directly(own_part, "tcol", 1)
    right_feats = broadcast_by_parts(left_feats, "trow", col_idx)
    tile_width = left_feats.shape[1]
    sub_rows = tile_width // n_dp
    gram_part = lax.psum_scatter(
        (
            lax.dot_general(left_feats, right_feats, contract, preferred_element_type=jnp.float32)
            / total_rows
        ).astype(jnp.bfloat16),
        "dp",
        scatter_dimension=0,
        tiled=True,
    ).astype(jnp.float32)
    global_rows = row_idx * tile_width + dp_idx * sub_rows + jnp.arange(sub_rows, dtype=jnp.int32)
    global_cols = col_idx * tile_width + jnp.arange(tile_width, dtype=jnp.int32)
    gram_rows = gram_part + RIDGE * (global_rows[:, None] == global_cols[None, :]).astype(
        jnp.float32
    )
    class_width = weights.shape[1]
    class_ids = row_idx * class_width + jnp.arange(class_width, dtype=jnp.int32)
    onehot = (labels[:, None] == class_ids[None, :]).astype(jnp.bfloat16)
    label_term = lax.dot_general(
        right_feats, onehot, contract, preferred_element_type=jnp.float32
    ) * (C / total_rows)
    label_rows = sum_at_owner(label_term.astype(jnp.bfloat16), "dp", 0)
    gram_three = gram_rows.astype(jnp.bfloat16).reshape(sub_rows, n_dp, sub_rows)
    block_ids = jnp.arange(n_row, dtype=jnp.int32)
    local_weights = weights.astype(jnp.bfloat16)[None]
    pieces = lax.all_gather(local_weights, ("trow", "dp"), axis=0, tiled=True)
    positions = jnp.arange(pieces.shape[0], dtype=jnp.int32)
    sub_index = positions % n_dp
    owner_index = positions // n_dp
    chosen = jnp.take(gram_three, sub_index, axis=1)
    products = jnp.einsum("rpk,pkc->rpc", chosen, pieces, preferred_element_type=jnp.float32)
    placing = (owner_index[:, None] == block_ids[None, :]).astype(jnp.float32)
    folded = jnp.einsum("rpc,pi->ric", products, placing)
    curv_local = folded.reshape(sub_rows, n_row * class_width)
    diag_block = lax.dynamic_slice_in_dim(gram_rows, dp_idx * sub_rows, sub_rows, 1)
    diag_local = jnp.diagonal(diag_block) * (row_idx == col_idx).astype(jnp.float32)
    row_total = of_everyone(curv_local.astype(jnp.bfloat16), "tcol").astype(jnp.float32)
    received, diag_vals = (
        broadcast(row_total.astype(jnp.bfloat16), "trow", col_idx).astype(row_total.dtype),
        broadcast(diag_local.astype(jnp.bfloat16), "trow", col_idx).astype(diag_local.dtype),
    )
    curv_mine = lax.dynamic_slice_in_dim(received, row_idx * class_width, class_width, 1)
    updated = weights - STEP_RATE * (curv_mine - label_rows) / diag_vals[:, None]
    return (gram_rows, updated)


def solution(mesh):
    return jax.shard_map(
        shards,
        mesh=mesh,
        in_specs=(
            P("dp", None),
            P(None, ("trow", "tcol")),
            P(("trow", "tcol")),
            P("dp"),
            P(("tcol", "dp"), "trow"),
        ),
        out_specs=(P(("trow", "dp"), "tcol"), P(("tcol", "dp"), "trow")),
        check_vma=False,
    )
```

profile of v0, /device:TPU:16, one launch (start us, length us, event | category | flops | bytes accessed | tf_op | source)
XLA Modules:
  0.0 348.0 jit_solution(17416006484841058802)
XLA Ops:
  8.0 1.6 copy-done
  9.6 3.3 fusion.5
  12.9 0.1 copy.15
  13.1 1.6 broadcast_in_dim.20
  14.7 6.1 %all-to-all-start = ((bf16[8,1024,128]{1,2,0:T(8,128)(2,1)}), bf16[8,1024,128]{1,2,0:T(8,128)(2,1)}, u32[]{:S(2)}, u32[]{:S(2)}) async-start(bf16[8,1024,128]{1,2,0:T(8,128)(2,1)} %broadcast_in_dim.20), calls=%async_computation | async-start | bytes 4194304 | tf_op jit(solution)/shard_map/all_to_all | solution.py:14
  20.9 27.0 %all-to-all-done = bf16[8,1024,128]{1,2,0:T(8,128)(2,1)} async-done(((bf16[8,1024,128]{1,2,0:T(8,128)(2,1)}), bf16[8,1024,128]{1,2,0:T(8,128)(2,1)}, u32[]{:S(2)}, u32[]{:S(2)}) %all-to-all-start) | async-done | bytes 2097184 | tf_op jit(solution)/shard_map/all_to_all | solution.py:14
  47.9 3.0 broadcast_select_fusion
  50.9 3.9 %copy.20 = bf16[1024,1024]{1,0:T(8,128)(2,1)} copy(bf16[1024,1024]{0,1:T(8,128)(2,1)} %broadcast_select_fusion) | data formatting | bytes 4194304
  55.0 45.5 %reduce-scatter.7.cloned.1.call-done = bf16[128,1024]{1,0:T(8,128)(2,1)} async-done(((bf16[1024,1024]{1,0:T(8,128)(2,1)}), bf16[128,1024]{1,0:T(8,128)(2,1)}) %reduce-scatter.7.cloned.1.call-update) | async-done | bytes 262160
  100.5 1.8 copy.21
  102.4 51.8 %all-gather.8.cloned.1.call-done = bf16[1024,1024]{0,1:T(8,128)(2,1)} async-done(((bf16[128,1024]{0,1:T(8,128)(2,1)}), bf16[1024,1024]{0,1:T(8,128)(2,1)}) %all-gather.8.cloned.1.call-update) | async-done | bytes 2097168 | tf_op jit(solution)/shard_map/all_gather | solution.py:43
  154.2 5.9 %multiply_convert_fusion = bf16[1024,1024]{1,0:T(8,128)(2,1)} fusion(bf16[1024,1024]{0,1:T(8,128)(2,1)} %bitcast.1, bf16[1024,1024]{0,1:T(8,128)(2,1)} %all-gather.8.cloned.1.call-done), kind=kOutput, calls=%fused_computation.2 | convolution fusion | flops 2149580800 | bytes 6291456 | tf_op jit(solution)/shard_map/dot_general | solution.py:88
  160.2 0.8 copy-done.2
  160.9 0.6 convert_element_type.73
  161.7 44.9 %reduce-scatter.5.cloned.1.call-done = bf16[128,1024]{1,0:T(8,128)(2,1)} async-done(((bf16[1024,1024]{1,0:T(8,128)(2,1)}), bf16[128,1024]{1,0:T(8,128)(2,1)}) %reduce-scatter.5.cloned.1.call-update) | async-done | bytes 262160 | tf_op jit(solution)/shard_map/reduce_scatter | solution.py:86
  206.6 1.1 convert_bitcast_fusion
  207.8 2.1 gather_fusion
  209.9 38.0 %all-gather.10.cloned.1.call-done = bf16[8192,125]{1,0:T(8,128)(2,1)} async-done(((bf16[128,125]{1,0:T(8,128)(2,1)}), bf16[8192,125]{1,0:T(8,128)(2,1)}) %all-gather.10.cloned.1.call-update) | async-done | bytes 2048016 | tf_op jit(solution)/shard_map/all_gather | solution.py:110
  247.9 4.3 %convolution_bitcast_fusion = bf16[128,64,125]{2,0,1:T(8,128)(2,1)} fusion(bf16[64,128,125]{2,1,0:T(8,128)(2,1)} %bitcast.56, bf16[64,128,128]{2,1,0:T(8,128)(2,1)} %gather_fusion, pred[64]{0:T(512)(128)(4,1)S(1)} %compare_and_fusion), kind=kOutput, calls=%fused_computation.3 | convolution fusion | flops 263192576 | bytes 6193216 | tf_op jit(solution)/shard_map/rpk,pkc->rpc/dot_general | solution.py:115
  252.2 4.1 %copy.17 = bf16[128,64,125]{0,1,2:T(8,128)(2,1)} copy(bf16[128,64,125]{2,0,1:T(8,128)(2,1)} %convolution_bitcast_fusion) | data formatting | bytes 4096000 | tf_op jit(solution)/shard_map/rpk,pkc->rpc/transpose | solution.py:115
  256.3 1.9 fusion.7
  258.4 0.3 broadcast_in_dim.27
  258.7 31.2 %all_to_all.15 = bf16[8,128,1000]{1,2,0:T(8,128)(2,1)} all-to-all(bf16[8,128,1000]{1,2,0:T(8,128)(2,1)S(1)} %broadcast_in_dim.27), channel_id=1, replica_groups=mesh['trow'=8,'tcol'=8,'dp'=8] {'tcol'}, dimensions={0} | all-to-all | bytes 4096000 | tf_op jit(solution)/shard_map/all_to_all | solution.py:14
  289.9 2.6 reduce_sum.21
  292.6 3.1 fusion.6
  295.7 3.9 %all-to-all-start.2 = ((bf16[8,128,125]{2,1,0:T(8,128)(2,1)}), bf16[8,128,125]{2,1,0:T(8,128)(2,1)S(1)}, u32[]{:S(2)}, u32[]{:S(2)}) async-start(bf16[8,128,125]{2,1,0:T(8,128)(2,1)} %bitcast.10), calls=%async_computation.3 | async-start | bytes 524288 | tf_op jit(solution)/shard_map/all_to_all | solution.py:54
  299.6 12.3 %all-to-all-done.2 = bf16[8,128,125]{2,1,0:T(8,128)(2,1)S(1)} async-done(((bf16[8,128,125]{2,1,0:T(8,128)(2,1)}), bf16[8,128,125]{2,1,0:T(8,128)(2,1)S(1)}, u32[]{:S(2)}, u32[]{:S(2)}) %all-to-all-start.2) | async-done | bytes 256032 | tf_op jit(solution)/shard_map/all_to_all | solution.py:54
  312.0 1.2 gather_fusion.1
  313.3 12.9 %all-gather.3 = bf16[8,1,128]{2,1,0:T(2,128)(2,1)S(1)} all-gather(bf16[1,1,128]{2,1,0:T(2,128)(2,1)S(1)} %convert_bitcast_fusion.1), channel_id=4, replica_groups=mesh['trow'=8,'tcol'=8,'dp'=8] {'trow'}, dimensions={0}, use_global_device_ids=true | all-gather | bytes 2304 | tf_op jit(solution)/shard_map/all_gather | solution.py:64
  326.1 11.7 %all-gather.12.cloned.1.call-done = bf16[1024,1000]{0,1:T(8,128)(2,1)} async-done(((bf16[128,1000]{0,1:T(8,128)(2,1)}), bf16[1024,1000]{0,1:T(8,128)(2,1)}) %all-gather.12.cloned.1.call-update) | async-done | bytes 2048016 | tf_op jit(solution)/shard_map/all_gather | solution.py:64
  337.8 2.2 copy.23
  340.2 0.7 fusion.14
  (33 shorter events, 0.8 us)
Async XLA Ops:
  8.0 1.6 copy-start
  14.7 33.2 %all-to-all-start = ((bf16[8,1024,128]{1,2,0:T(8,128)(2,1)}), bf16[8,1024,128]{1,2,0:T(8,128)(2,1)}, u32[]{:S(2)}, u32[]{:S(2)}) async-start(bf16[8,1024,128]{1,2,0:T(8,128)(2,1)} %broadcast_in_dim.20), calls=%async_computation | async-start | bytes 4194304 | tf_op jit(solution)/shard_map/all_to_all | solution.py:14
  20.8 79.7 %reduce-scatter.7.cloned.1.call-start = ((), (), s32[]{:S(2)}) async-start(), calls=%async_computation.9 | async-start | bytes 2359296
  54.9 99.3 %all-gather.8.cloned.1.call-start = ((), (), s32[]{:S(2)}) async-start(), calls=%async_computation.5 | async-start | bytes 2359296 | tf_op jit(solution)/shard_map/all_gather | solution.py:43
  102.3 104.3 %reduce-scatter.5.cloned.1.call-start = ((), (), s32[]{:S(2)}) async-start(), calls=%async_computation.6 | async-start | bytes 2359296 | tf_op jit(solution)/shard_map/reduce_scatter | solution.py:86
  160.1 0.8 copy-start.2
  160.1 87.8 %all-gather.10.cloned.1.call-start = ((), (), s32[]{:S(2)}) async-start(), calls=%async_computation.7 | async-start | bytes 2129920 | tf_op jit(solution)/shard_map/all_gather | solution.py:110
  161.6 176.2 %all-gather.12.cloned.1.call-start = ((), (), s32[]{:S(2)}) async-start(), calls=%async_computation.8 | async-start | bytes 2304000 | tf_op jit(solution)/shard_map/all_gather | solution.py:64
  207.7 104.3 %copy-start.1 = (f32[128,1024]{1,0:T(8,128)}, f32[128,1024]{1,0:T(8,128)S(1)}, u32[]{:S(2)}) copy-start(f32[128,1024]{1,0:T(8,128)S(1)} %get-tuple-element.3) | copy-start | bytes 1572868
  289.9 2.7 copy-start.3
  295.7 16.2 %all-to-all-start.2 = ((bf16[8,128,125]{2,1,0:T(8,128)(2,1)}), bf16[8,128,125]{2,1,0:T(8,128)(2,1)S(1)}, u32[]{:S(2)}, u32[]{:S(2)}) async-start(bf16[8,128,125]{2,1,0:T(8,128)(2,1)} %bitcast.10), calls=%async_computation.3 | async-start | bytes 524288 | tf_op jit(solution)/shard_map/all_to_all | solution.py:54
Sparse Core Ops, SparseCore 0:
  55.0 45.4 reduce-scatter.6
  103.1 51.0 all-gather.7
  160.2 46.2 reduce-scatter.4
  292.7 45.1 all-gather.11
Sparse Core Ops, SparseCore 1:
  164.5 83.4 all-gather.9
where the time goes:
time: 349 us; the launch traced here: 348 us
  waiting for transfers between devices  231 us (66%)
  blocking collectives  44.1 us (13%)
  local copies, waits for them, and re-layouts  20.1 us (6%)
  matrix products  18.6 us (5%)
  between operations  15.4 us (4%)
  starting transfers between devices  10.2 us (3%)
  other arithmetic  8.31 us (2%)
    all_gather x1, waiting for transfers between devices, broadcast_by_parts(): lax.all_gather(own, axis, axis=0, tiled=True)[:len(lines)]  51.8 us
    unnamed x6, waiting for transfers between devices  45.6 us
    reduce_scatter x1, waiting for transfers between devices, shards(): lax.psum_scatter((lax.dot_general(left_feats, right_feats, contract, pref...  44.9 us
    all_gather x1, waiting for transfers between devices, shards(): pieces = lax.all_gather(local_weights, ('trow', 'dp'), axis=0, tiled=True)  38 us
    all_to_all x1, blocking collectives, copy_for_each(): lax.all_to_all(jnp.broadcast_to(array[None], (size, *array.shape)), axis,...  31.2 us
    all_to_all x1, waiting for transfers between devices, copy_for_each(): lax.all_to_all(jnp.broadcast_to(array[None], (size, *array.shape)), axis,...  27 us
    all_gather x1, blocking collectives, broadcast(): lax.all_gather(array, axis)  12.9 us
    all_to_all x1, waiting for transfers between devices, sum_at_owner(): lax.all_to_all(parts, axis, split_axis=0, concat_axis=0, tiled=True)  12.3 us
  transfers between devices with their start and end apart: 7, of which 7 were waited for; matrix products, arithmetic and copies ran while one was open for 2% of the time, Pallas kernels for 0%

commit v1 on v0

--- a/solution.py
+++ b/solution.py
@@ -40,7 +40,9 @@
     )
     padded = padded_to(lines, lax.axis_size(axis))
     own = lax.psum_scatter(padded, axis, scatter_dimension=0, tiled=True)
-    return lax.all_gather(own, axis, axis=0, tiled=True)[: len(lines)].reshape(array.shape)
+    return jnp.concatenate(
+        lax.all_to_all(jnp.stack([own] * lax.axis_size(axis)), axis, 0, 0), axis=0
+    )[: len(lines)].reshape(array.shape)
 
 
 def split_up(array, dim, size):

time: 349 us -> 348 us (level)
  waiting for transfers between devices: 231 us -> 180 us
  blocking collectives: 44.1 us -> 94.9 us
    all_gather x1 -> x0, waiting for transfers between devices: 51.8 us -> none  [broadcast_by_parts(): lax.all_gather(own, axis, axis=0, tiled=True)[:len(lines)]]
    all_to_all x0 -> x1, blocking collectives: none -> 50.9 us  [broadcast_by_parts(): lax.all_to_all(jnp.stack([own] * lax.axis_size(axis)), axis, 0, 0)]
    unnamed x6 -> x4, waiting for transfers between devices: 45.6 us -> 0.07 us
    reduce_scatter x0 -> x1, waiting for transfers between devices: none -> 45.5 us  [broadcast_by_parts(): own = lax.psum_scatter(padded, axis, scatter_dimension=0, tiled=True)]
    unnamed x11 -> x12, local copies, waits for them, and re-layouts: 10.3 us -> 9.81 us
  transfers between devices with their start and end apart: 7 -> 6, of which waited for: 7 -> 6; matrix products, arithmetic and copies ran while one was open for 2% -> 2% of each run, Pallas kernels for 0% -> 0%
where the time goes in v1:
time: 348 us; the launch traced here: 347 us
  waiting for transfers between devices  180 us (52%)
  blocking collectives  94.9 us (27%)
  local copies, waits for them, and re-layouts  20.8 us (6%)
  matrix products  18.1 us (5%)
  between operations  15.4 us (4%)
  starting transfers between devices  10.2 us (3%)
  other arithmetic  8.31 us (2%)
    all_to_all x1, blocking collectives, broadcast_by_parts(): lax.all_to_all(jnp.stack([own] * lax.axis_size(axis)), axis, 0, 0)  50.9 us
    reduce_scatter x1, waiting for transfers between devices, broadcast_by_parts(): own = lax.psum_scatter(padded, axis, scatter_dimension=0, tiled=True)  45.5 us
    reduce_scatter x1, waiting for transfers between devices, shards(): lax.psum_scatter((lax.dot_general(left_feats, right_feats, contract, pref...  45.1 us
    all_gather x1, waiting for transfers between devices, shards(): pieces = lax.all_gather(local_weights, ('trow', 'dp'), axis=0, tiled=True)  38.1 us
    all_to_all x1, blocking collectives, copy_for_each(): lax.all_to_all(jnp.broadcast_to(array[None], (size, *array.shape)), axis,...  31.2 us
    all_to_all x1, waiting for transfers between devices, copy_for_each(): lax.all_to_all(jnp.broadcast_to(array[None], (size, *array.shape)), axis,...  27 us
    all_gather x1, blocking collectives, broadcast(): lax.all_gather(array, axis)  12.9 us
    all_to_all x1, waiting for transfers between devices, sum_at_owner(): lax.all_to_all(parts, axis, split_axis=0, concat_axis=0, tiled=True)  12.3 us
  transfers between devices with their start and end apart: 6, of which 6 were waited for; matrix products, arithmetic and copies ran while one was open for 2% of the time, Pallas kernels for 0%

profile of v1, /device:TPU:16, one launch (start us, length us, event | category | flops | bytes accessed | tf_op | source)
XLA Modules:
  0.0 347.4 jit_solution(7969147184682010999)
XLA Ops:
  8.0 1.6 copy-done
  9.6 3.3 fusion.5
  13.1 1.6 broadcast_in_dim.20
  14.7 6.1 %all-to-all-start = ((bf16[8,1024,128]{1,2,0:T(8,128)(2,1)}), bf16[8,1024,128]{1,2,0:T(8,128)(2,1)}, u32[]{:S(2)}, u32[]{:S(2)}) async-start(bf16[8,1024,128]{1,2,0:T(8,128)(2,1)} %broadcast_in_dim.20), calls=%async_computation | async-start | bytes 4194304 | tf_op jit(solution)/shard_map/all_to_all | solution.py:14
  20.9 27.0 %all-to-all-done = bf16[8,1024,128]{1,2,0:T(8,128)(2,1)} async-done(((bf16[8,1024,128]{1,2,0:T(8,128)(2,1)}), bf16[8,1024,128]{1,2,0:T(8,128)(2,1)}, u32[]{:S(2)}, u32[]{:S(2)}) %all-to-all-start) | async-done | bytes 2097184 | tf_op jit(solution)/shard_map/all_to_all | solution.py:14
  47.9 3.1 broadcast_select_fusion
  51.0 3.9 %copy.23 = bf16[1024,1024]{1,0:T(8,128)(2,1)} copy(bf16[1024,1024]{0,1:T(8,128)(2,1)} %broadcast_select_fusion) | data formatting | bytes 4194304
  55.0 45.5 %reduce-scatter.7.cloned.1.call-done = bf16[128,1024]{1,0:T(8,128)(2,1)} async-done(((bf16[1024,1024]{1,0:T(8,128)(2,1)}), bf16[128,1024]{1,0:T(8,128)(2,1)}) %reduce-scatter.7.cloned.1.call-update) | async-done | bytes 262160 | tf_op jit(solution)/shard_map/reduce_scatter | solution.py:42
  100.5 1.2 stack.2
  101.7 50.9 %all_to_all.20 = bf16[8,128,1024]{2,1,0:T(8,128)(2,1)S(1)} all-to-all(bf16[8,128,1024]{2,1,0:T(8,128)(2,1)S(1)} %stack.2), channel_id=1, replica_groups=mesh['trow'=8,'tcol'=8,'dp'=8] {'trow'}, dimensions={0} | all-to-all | bytes 4194304 | tf_op jit(solution)/shard_map/all_to_all | solution.py:44
  152.6 1.3 copy-done.1
  153.9 5.3 %multiply_convert_fusion = bf16[1024,1024]{1,0:T(8,128)(2,1)} fusion(bf16[1024,1024]{0,1:T(8,128)(2,1)} %bitcast.1, bf16[1024,1024]{1,0:T(8,128)(2,1)S(1)} %bitcast.58), kind=kOutput, calls=%fused_computation.2 | convolution fusion | flops 2149580800 | bytes 6291456 | tf_op jit(solution)/shard_map/dot_general | solution.py:90
  159.3 0.8 copy-done.3
  160.0 0.6 convert_element_type.73
  160.8 45.1 %reduce-scatter.5.cloned.1.call-done = bf16[128,1024]{1,0:T(8,128)(2,1)} async-done(((bf16[1024,1024]{1,0:T(8,128)(2,1)}), bf16[128,1024]{1,0:T(8,128)(2,1)}) %reduce-scatter.5.cloned.1.call-update) | async-done | bytes 262160 | tf_op jit(solution)/shard_map/reduce_scatter | solution.py:88
  205.9 1.1 convert_bitcast_fusion
  207.0 2.2 gather_fusion
  209.2 38.1 %all-gather.7.cloned.1.call-done = bf16[8192,125]{1,0:T(8,128)(2,1)} async-done(((bf16[128,125]{1,0:T(8,128)(2,1)}), bf16[8192,125]{1,0:T(8,128)(2,1)}) %all-gather.7.cloned.1.call-update) | async-done | bytes 2048016 | tf_op jit(solution)/shard_map/all_gather | solution.py:112
  247.3 4.3 %convolution_bitcast_fusion = bf16[128,64,125]{2,0,1:T(8,128)(2,1)} fusion(bf16[64,128,125]{2,1,0:T(8,128)(2,1)} %bitcast.57, bf16[64,128,128]{2,1,0:T(8,128)(2,1)} %gather_fusion, pred[64]{0:T(512)(128)(4,1)S(1)} %compare_and_fusion), kind=kOutput, calls=%fused_computation.3 | convolution fusion | flops 263192576 | bytes 6193216 | tf_op jit(solution)/shard_map/rpk,pkc->rpc/dot_general | solution.py:117
  251.6 4.1 %copy.20 = bf16[128,64,125]{0,1,2:T(8,128)(2,1)} copy(bf16[128,64,125]{2,0,1:T(8,128)(2,1)} %convolution_bitcast_fusion) | data formatting | bytes 4096000 | tf_op jit(solution)/shard_map/rpk,pkc->rpc/transpose | solution.py:117
  255.7 1.9 fusion.7
  257.8 0.3 broadcast_in_dim.27
  258.0 31.2 %all_to_all.21 = bf16[8,128,1000]{1,2,0:T(8,128)(2,1)} all-to-all(bf16[8,128,1000]{1,2,0:T(8,128)(2,1)S(1)} %broadcast_in_dim.27), channel_id=1, replica_groups=mesh['trow'=8,'tcol'=8,'dp'=8] {'tcol'}, dimensions={0} | all-to-all | bytes 4096000 | tf_op jit(solution)/shard_map/all_to_all | solution.py:14
  289.2 2.6 reduce_sum.21
  291.9 3.3 fusion.6
  295.2 3.9 %all-to-all-start.3 = ((bf16[8,128,125]{2,1,0:T(8,128)(2,1)}), bf16[8,128,125]{2,1,0:T(8,128)(2,1)S(1)}, u32[]{:S(2)}, u32[]{:S(2)}) async-start(bf16[8,128,125]{2,1,0:T(8,128)(2,1)} %bitcast.11), calls=%async_computation.4 | async-start | bytes 524288 | tf_op jit(solution)/shard_map/all_to_all | solution.py:56
  299.1 12.3 %all-to-all-done.3 = bf16[8,128,125]{2,1,0:T(8,128)(2,1)S(1)} async-done(((bf16[8,128,125]{2,1,0:T(8,128)(2,1)}), bf16[8,128,125]{2,1,0:T(8,128)(2,1)S(1)}, u32[]{:S(2)}, u32[]{:S(2)}) %all-to-all-start.3) | async-done | bytes 256032 | tf_op jit(solution)/shard_map/all_to_all | solution.py:56
  311.5 1.2 gather_fusion.1
  312.7 12.9 %all-gather.3 = bf16[8,1,128]{2,1,0:T(2,128)(2,1)S(1)} all-gather(bf16[1,1,128]{2,1,0:T(2,128)(2,1)S(1)} %convert_bitcast_fusion.1), channel_id=4, replica_groups=mesh['trow'=8,'tcol'=8,'dp'=8] {'trow'}, dimensions={0}, use_global_device_ids=true | all-gather | bytes 2304 | tf_op jit(solution)/shard_map/all_gather | solution.py:66
  325.6 11.6 %all-gather.9.cloned.1.call-done = bf16[1024,1000]{0,1:T(8,128)(2,1)} async-done(((bf16[128,1000]{0,1:T(8,128)(2,1)}), bf16[1024,1000]{0,1:T(8,128)(2,1)}) %all-gather.9.cloned.1.call-update) | async-done | bytes 2048016 | tf_op jit(solution)/shard_map/all_gather | solution.py:66
  337.2 2.2 copy.26
  339.5 0.7 fusion.14
  (33 shorter events, 0.9 us)
Async XLA Ops:
  8.0 1.6 copy-start
  14.7 33.2 %all-to-all-start = ((bf16[8,1024,128]{1,2,0:T(8,128)(2,1)}), bf16[8,1024,128]{1,2,0:T(8,128)(2,1)}, u32[]{:S(2)}, u32[]{:S(2)}) async-start(bf16[8,1024,128]{1,2,0:T(8,128)(2,1)} %broadcast_in_dim.20), calls=%async_computation | async-start | bytes 4194304 | tf_op jit(solution)/shard_map/all_to_all | solution.py:14
  20.8 79.7 %reduce-scatter.7.cloned.1.call-start = ((), (), s32[]{:S(2)}) async-start(), calls=%async_computation.9 | async-start | bytes 2359296 | tf_op jit(solution)/shard_map/reduce_scatter | solution.py:42
  54.9 150.9 %reduce-scatter.5.cloned.1.call-start = ((), (), s32[]{:S(2)}) async-start(), calls=%async_computation.6 | async-start | bytes 2359296 | tf_op jit(solution)/shard_map/reduce_scatter | solution.py:88
  152.6 1.3 copy-start.1
  159.2 0.8 copy-start.3
  159.2 88.1 %all-gather.7.cloned.1.call-start = ((), (), s32[]{:S(2)}) async-start(), calls=%async_computation.7 | async-start | bytes 2129920 | tf_op jit(solution)/shard_map/all_gather | solution.py:112
  160.7 176.5 %all-gather.9.cloned.1.call-start = ((), (), s32[]{:S(2)}) async-start(), calls=%async_computation.8 | async-start | bytes 2304000 | tf_op jit(solution)/shard_map/all_gather | solution.py:66
  207.0 104.5 %copy-start.2 = (f32[128,1024]{1,0:T(8,128)}, f32[128,1024]{1,0:T(8,128)S(1)}, u32[]{:S(2)}) copy-start(f32[128,1024]{1,0:T(8,128)S(1)} %get-tuple-element.3) | copy-start | bytes 1572868
  289.2 2.7 copy-start.4
  295.2 16.2 %all-to-all-start.3 = ((bf16[8,128,125]{2,1,0:T(8,128)(2,1)}), bf16[8,128,125]{2,1,0:T(8,128)(2,1)S(1)}, u32[]{:S(2)}, u32[]{:S(2)}) async-start(bf16[8,128,125]{2,1,0:T(8,128)(2,1)} %bitcast.11), calls=%async_computation.4 | async-start | bytes 524288 | tf_op jit(solution)/shard_map/all_to_all | solution.py:56
Sparse Core Ops, SparseCore 0:
  55.0 45.4 reduce-scatter.6
  159.3 46.4 reduce-scatter.4
  292.0 45.1 all-gather.8
Sparse Core Ops, SparseCore 1:
  163.6 83.6 all-gather.6
